TPU v7x, 512 devices: a whole 4x8x8 slice. The times are simulated.
512 devices in a mesh: ab: 16 (over x, z_lo), cd: 32 (over y, z_hi, core).
Axes of the slice: x: 4, y: 8, z: 8 (z_hi: 2, z_lo: 4; z = z_hi * 4 + z_lo), core: 2. Of those that a mesh axis runs over, the one named last changes fastest.
Arguments:
- amplitudes: float32 [576, 25600], P('ab', 'cd'), may hold values from -6 to 6
- integrals: float32 [16384, 25600], P('ab', 'cd'), may hold values from -0.0390625 to 0.0390625
- occupied_energy: float32 [24], replicated, may hold values from -2 to -0.4
- virtual_energy: float32 [128], replicated, may hold values from 0.3 to 3
Outputs:
- update: float32 [576, 16384], P('cd', 'ab')
All inputs are finite; a program needn't handle non-finite values.
Results may differ from a plain program's by a relative error of at most 0.000071.
Values sent between devices are 32-bit elements; how exact they have to be, the bound alone decides.
A program may use at most 64 MiB of HBM per device.

v0:
```python
import jax
import jax.numpy as jnp
from jax import lax
from jax.sharding import PartitionSpec as P

AW = 128
NO = 24


def body(amplitudes, integrals, occupied_energy, virtual_energy):
    owned_pairs = integrals.shape[0]
    owned_first = owned_pairs // AW
    pair_count = NO * NO
    partial_value = lax.dot_general(
        lax.all_gather(amplitudes, "ab", axis=0, tiled=True),
        integrals,
        (((1,), (1,)), ((), ())),
        precision=lax.Precision.HIGHEST,
        preferred_element_type=jnp.float32,
    )
    blocks = partial_value.reshape(pair_count, owned_first, AW)
    turned = lax.all_to_all(blocks, "ab", split_axis=2, concat_axis=1, tiled=True)
    flipped = jnp.transpose(turned.reshape(NO, NO, AW, owned_first), (1, 0, 3, 2)).reshape(
        pair_count, owned_pairs
    )
    combined = partial_value + flipped
    summed = lax.psum_scatter(combined, "cd", scatter_dimension=0, tiled=True)
    local_rows = summed.shape[0]
    first_index = lax.axis_index("cd") * local_rows
    row_index = first_index + lax.iota(jnp.int32, local_rows)
    orbital_ids = lax.iota(jnp.int32, NO)
    select_first = (row_index[:, None] // NO == orbital_ids[None, :]).astype(jnp.float32)
    select_second = (row_index[:, None] % NO == orbital_ids[None, :]).astype(jnp.float32)
    occ_sum = jnp.sum((select_first + select_second) * occupied_energy[None, :], axis=1)
    owned_virtual = lax.dynamic_slice_in_dim(
        virtual_energy, lax.axis_index("ab") * owned_first, owned_first, 0
    )
    denominator = (
        owned_virtual[None, :, None] + virtual_energy[None, None, :] - occ_sum[:, None, None]
    )
    result = summed.reshape(local_rows, owned_first, AW) / denominator
    return result.reshape(local_rows, owned_pairs)


def solution(mesh):
    return jax.shard_map(
        body,
        mesh=mesh,
        in_specs=(P("ab", "cd"), P("ab", "cd"), P(), P()),
        out_specs=P("cd", "ab"),
        check_vma=False,
    )
```

profile of v0, /device:TPU:19, one launch (start us, length us, event | category | flops | bytes accessed | tf_op | source)
XLA Modules:
  0.0 381.9 jit_solution(14902521364361258140)
XLA Ops:
  6.5 0.7 all-gather.3.cloned.1.call-update
  7.3 83.8 %all-gather.3.cloned.1.call-done = f32[16,36,800]{2,1,0:T(8,128)} async-done(((f32[1,36,800]{2,1,0:T(8,128)}), f32[16,36,800]{2,1,0:T(8,128)}) %all-gather.3.cloned.1.call-update) | async-done | bytes 1843216 | tf_op jit(solution)/shard_map/all_gather | solution.py:15
  91.1 2.7 reshape.80
  93.8 9.2 %fusion.2 = f32[576,1024]{1,0:T(8,128)S(1)} fusion(f32[576,800]{1,0:T(8,128)} %reshape.80, f32[1024,800]{0,1:T(8,128)S(1)} %copy-done), kind=kOutput, calls=%fused_computation.10 | convolution fusion | flops 5662310400 | bytes 7479296 | tf_op jit(solution)/shard_map/dot_general | solution.py:14
  103.0 2.1 copy.17
  105.1 3.5 copy.12
  108.6 11.0 %all-to-all-start = ((f32[576,8,128]{0,1,2:T(8,128)}), f32[576,8,128]{0,1,2:T(8,128)}, u32[]{:S(2)}, u32[]{:S(2)}) async-start(f32[576,8,128]{0,1,2:T(8,128)} %copy.12), calls=%async_computation | async-start | bytes 5242880 | tf_op jit(solution)/shard_map/all_to_all | solution.py:22
  119.6 0.1 dynamic_slice.3
  119.7 1.3 dynamic-slice.4
  121.6 0.1 add.65
  121.7 54.3 %all-to-all-done = f32[576,8,128]{0,1,2:T(8,128)} async-done(((f32[576,8,128]{0,1,2:T(8,128)}), f32[576,8,128]{0,1,2:T(8,128)}, u32[]{:S(2)}, u32[]{:S(2)}) %all-to-all-start) | async-done | bytes 2359328 | tf_op jit(solution)/shard_map/all_to_all | solution.py:22
  176.0 3.7 copy.14
  179.6 9.1 %reshape.77 = f32[24,24,128,8]{1,0,3,2:T(8,128)} reshape(f32[576,16,8,8]{0,3,2,1:T(8,128)} %copy.14) | data formatting | bytes 4718592 | tf_op jit(solution)/shard_map/reshape | solution.py:23
  188.7 10.3 %copy.15 = f32[24,24,8,128]{3,2,1,0:T(8,128)} copy(f32[24,24,8,128]{0,1,2,3:T(8,128)} %bitcast.23) | data formatting | bytes 4718592 | tf_op jit(solution)/shard_map/transpose | solution.py:23
  199.0 4.6 %bitcast_add_fusion = f32[576,1024]{1,0:T(8,128)} fusion(f32[576,1024]{1,0:T(8,128)} %copy-done.1, f32[72,8,8,128]{3,2,1,0:T(8,128)} %bitcast.25), kind=kLoop, calls=%fused_computation | loop fusion | flops 589824 | bytes 7077888 | tf_op jit(solution)/shard_map/add | solution.py:26
  203.6 105.0 %fusion = f32[24,1024]{1,0:T(8,128)S(1)} fusion(f32[576,1024]{1,0:T(8,128)} %bitcast_add_fusion), kind=kCustom, calls=%all-reduce-scatter | all-reduce-scatter fusion | flops 786433 | bytes 2459648
  308.7 8.1 %collective-permute-start = (f32[24,1024]{1,0:T(8,128)S(1)}, f32[24,1024]{1,0:T(8,128)S(1)}, u32[]{:S(2)}, u32[]{:S(2)}) collective-permute-start(f32[24,1024]{1,0:T(8,128)S(1)} %fusion), channel_id=1, source_target_pairs={{0,1},{1,2},{2,3},{3,4},{4,5},{5,6},{6,7},{7,8},{8,9},{9,10},{10,1... | collective-permute-start | bytes 294920
  316.8 3.3 collective-permute-start.1
  320.1 1.9 collective-permute-start.7
  322.0 2.2 collective-permute-start.2
  324.2 6.7 %collective-permute-start.3 = (f32[24,1024]{1,0:T(8,128)S(1)}, f32[24,1024]{1,0:T(8,128)S(1)}, u32[]{:S(2)}, u32[]{:S(2)}) collective-permute-start(f32[24,1024]{1,0:T(8,128)S(1)} %fusion), channel_id=1, source_target_pairs={{0,4},{1,5},{2,6},{3,7},{4,8},{5,9},{6,10},{7,11},{8,12},{9,13},{1... | collective-permute-start | bytes 294920
  330.9 0.0 copy-start.3
  330.9 10.5 %collective-permute-start.4 = (f32[24,1024]{1,0:T(8,128)S(1)}, f32[24,1024]{1,0:T(8,128)S(1)}, u32[]{:S(2)}, u32[]{:S(2)}) collective-permute-start(f32[24,1024]{1,0:T(8,128)S(1)} %fusion), channel_id=1, source_target_pairs={{0,5},{1,6},{2,7},{3,8},{4,9},{5,10},{6,11},{7,12},{8,13},{9,14},{... | collective-permute-start | bytes 294920
  341.4 6.4 %collective-permute-start.5 = (f32[24,1024]{1,0:T(8,128)S(1)}, f32[24,1024]{1,0:T(8,128)S(1)}, u32[]{:S(2)}, u32[]{:S(2)}) collective-permute-start(f32[24,1024]{1,0:T(8,128)S(1)} %fusion), channel_id=1, source_target_pairs={{0,6},{1,7},{2,8},{3,9},{4,10},{5,11},{6,12},{7,13},{8,14},{9,15},... | collective-permute-start | bytes 294920
  347.8 0.0 collective-permute-done.1
  347.8 1.9 collective-permute-start.6
  349.7 0.2 multiply_reduce_fusion
  350.0 2.6 collective-permute-done.5
  352.6 0.6 copy-done.7
  353.3 6.3 %collective-permute-done.6 = f32[24,1024]{1,0:T(8,128)} collective-permute-done((f32[24,1024]{1,0:T(8,128)S(1)}, f32[24,1024]{1,0:T(8,128)}, u32[]{:S(2)}, u32[]{:S(2)}) %collective-permute-start.6) | collective-permute-done | bytes 98336
  359.5 13.9 %concatenate = f32[210,1024]{1,0:T(8,128)} concatenate(f32[18,1024]{1,0:T(8,128)} %copy-done.3, f32[24,1024]{1,0:T(8,128)} %collective-permute-done.6, f32[24,1024]{1,0:T(8,128)} %copy-done.7, f32[24,1024]{1,0:T(8,128)} %copy-done.6, f32[24,1024]{1,0:T(8,128)} %copy-done.5, f32[24,1024]{1,0:T(8,128)} %copy-done.4, f32[24,1024]{1,0:T(8,128)} %copy-done.2, ...), dimensions={0} | concatenate | bytes 1720320
  373.4 1.6 dynamic-slice_divide_fusion
  (27 shorter events, 0.1 us)
Async XLA Ops:
  6.5 87.2 %copy-start = (f32[1024,800]{0,1:T(8,128)S(1)}, f32[1024,800]{0,1:T(8,128)}, u32[]{:S(2)}) copy-start(f32[1024,800]{0,1:T(8,128)} %param.5) | copy-start | bytes 9830404
  6.5 84.6 %all-gather.3.cloned.1.call-start = ((), (), s32[]{:S(2)}) async-start(), calls=%async_computation.1 | async-start | bytes 2437120 | tf_op jit(solution)/shard_map/all_gather | solution.py:15
  103.0 2.1 copy-start.1
  108.6 11.0 %copy-start.8 = (f32[128]{0:T(128)S(1)}, f32[128]{0:T(128)}, u32[]{:S(2)}) copy-start(f32[128]{0:T(128)} %param.7) | copy-start | bytes 1540
  108.6 67.4 %all-to-all-start = ((f32[576,8,128]{0,1,2:T(8,128)}), f32[576,8,128]{0,1,2:T(8,128)}, u32[]{:S(2)}, u32[]{:S(2)}) async-start(f32[576,8,128]{0,1,2:T(8,128)} %copy.12), calls=%async_computation | async-start | bytes 5242880 | tf_op jit(solution)/shard_map/all_to_all | solution.py:22
  203.6 146.1 %copy-start.9 = (f32[24]{0:T(128)S(1)}, f32[24]{0:T(128)}, u32[]{:S(2)}) copy-start(f32[24]{0:T(128)} %param.6) | copy-start | bytes 292
  308.7 32.7 %collective-permute-start = (f32[24,1024]{1,0:T(8,128)S(1)}, f32[24,1024]{1,0:T(8,128)S(1)}, u32[]{:S(2)}, u32[]{:S(2)}) collective-permute-start(f32[24,1024]{1,0:T(8,128)S(1)} %fusion), channel_id=1, source_target_pairs={{0,1},{1,2},{2,3},{3,4},{4,5},{5,6},{6,7},{7,8},{8,9},{9,10},{10,1... | collective-permute-start | bytes 294920
  316.8 31.0 %collective-permute-start.1 = (f32[24,1024]{1,0:T(8,128)S(1)}, f32[24,1024]{1,0:T(8,128)S(1)}, u32[]{:S(2)}, u32[]{:S(2)}) collective-permute-start(f32[24,1024]{1,0:T(8,128)S(1)} %fusion), channel_id=1, source_target_pairs={{0,2},{1,3},{2,4},{3,5},{4,6},{5,7},{6,8},{7,9},{8,10},{9,11},{10,... | collective-permute-start | bytes 294920
  320.1 10.8 %collective-permute-start.7 = (f32[18,1024]{1,0:T(8,128)S(1)}, f32[18,1024]{1,0:T(8,128)S(1)}, u32[]{:S(2)}, u32[]{:S(2)}) collective-permute-start(f32[18,1024]{1,0:T(8,128)S(1)} %slice), channel_id=1, source_target_pairs={{0,8},{1,9},{2,10},{3,11},{4,12},{5,13},{6,14},{7,15},{8,16},{9,17... | collective-permute-start | bytes 221192
  322.0 27.9 %collective-permute-start.2 = (f32[24,1024]{1,0:T(8,128)S(1)}, f32[24,1024]{1,0:T(8,128)S(1)}, u32[]{:S(2)}, u32[]{:S(2)}) collective-permute-start(f32[24,1024]{1,0:T(8,128)S(1)} %fusion), channel_id=1, source_target_pairs={{0,3},{1,4},{2,5},{3,6},{4,7},{5,8},{6,9},{7,10},{8,11},{9,12},{10... | collective-permute-start | bytes 294920
  324.2 25.7 %collective-permute-start.3 = (f32[24,1024]{1,0:T(8,128)S(1)}, f32[24,1024]{1,0:T(8,128)S(1)}, u32[]{:S(2)}, u32[]{:S(2)}) collective-permute-start(f32[24,1024]{1,0:T(8,128)S(1)} %fusion), channel_id=1, source_target_pairs={{0,4},{1,5},{2,6},{3,7},{4,8},{5,9},{6,10},{7,11},{8,12},{9,13},{1... | collective-permute-start | bytes 294920
  330.9 21.7 %copy-start.3 = (f32[18,1024]{1,0:T(8,128)}, f32[18,1024]{1,0:T(8,128)S(1)}, u32[]{:S(2)}) copy-start(f32[18,1024]{1,0:T(8,128)S(1)} %collective-permute-done.7) | copy-start | bytes 221188
  330.9 19.0 %collective-permute-start.4 = (f32[24,1024]{1,0:T(8,128)S(1)}, f32[24,1024]{1,0:T(8,128)S(1)}, u32[]{:S(2)}, u32[]{:S(2)}) collective-permute-start(f32[24,1024]{1,0:T(8,128)S(1)} %fusion), channel_id=1, source_target_pairs={{0,5},{1,6},{2,7},{3,8},{4,9},{5,10},{6,11},{7,12},{8,13},{9,14},{... | collective-permute-start | bytes 294920
  341.4 11.2 %collective-permute-start.5 = (f32[24,1024]{1,0:T(8,128)S(1)}, f32[24,1024]{1,0:T(8,128)S(1)}, u32[]{:S(2)}, u32[]{:S(2)}) collective-permute-start(f32[24,1024]{1,0:T(8,128)S(1)} %fusion), channel_id=1, source_target_pairs={{0,6},{1,7},{2,8},{3,9},{4,10},{5,11},{6,12},{7,13},{8,14},{9,15},... | collective-permute-start | bytes 294920
  347.8 4.8 %copy-start.2 = (f32[24,1024]{1,0:T(8,128)}, f32[24,1024]{1,0:T(8,128)S(1)}, u32[]{:S(2)}) copy-start(f32[24,1024]{1,0:T(8,128)S(1)} %collective-permute-done.1) | copy-start | bytes 294916
  347.8 11.7 %collective-permute-start.6 = (f32[24,1024]{1,0:T(8,128)S(1)}, f32[24,1024]{1,0:T(8,128)}, u32[]{:S(2)}, u32[]{:S(2)}) collective-permute-start(f32[24,1024]{1,0:T(8,128)S(1)} %fusion), channel_id=1, source_target_pairs={{0,7},{1,8},{2,9},{3,10},{4,11},{5,12},{6,13},{7,14},{8,15},{9,16}... | collective-permute-start | bytes 294920
  349.9 2.7 copy-start.4
  350.0 2.7 copy-start.5
  350.0 2.7 copy-start.6
  352.6 0.6 copy-start.7
Sparse Core Ops, SparseCore 0:
  9.4 81.6 all-gather.2
where the time goes:
time: 383 us; the launch traced here: 382 us
  waiting for transfers between devices  148 us (39%)
  blocking collectives  105 us (27%)
  starting transfers between devices  51.9 us (14%)
  local copies, waits for them, and re-layouts  47.3 us (12%)
  between operations  14.3 us (4%)
  matrix products  9.21 us (2%)
  other arithmetic  6.46 us (2%)
    unnamed x1, blocking collectives  105 us
    all_gather x1, waiting for transfers between devices, body(): lax.all_gather(amplitudes, 'ab', axis=0, tiled=True)  83.8 us
    all_to_all x1, waiting for transfers between devices, body(): lax.all_to_all(blocks, 'ab', split_axis=2, concat_axis=1, tiled=True)  54.3 us
    unnamed x8, starting transfers between devices  40.9 us
    unnamed x25, local copies, waits for them, and re-layouts  20.6 us
    all_to_all x1, starting transfers between devices, body(): lax.all_to_all(blocks, 'ab', split_axis=2, concat_axis=1, tiled=True)  11 us
    transpose x1, local copies, waits for them, and re-layouts, body(): jnp.transpose(turned.reshape(NO, NO, AW, owned_first), (1, 0, 3, 2))  10.3 us
    unnamed x9, waiting for transfers between devices  9.63 us
  transfers between devices with their start and end apart: 10, of which 4 were waited for; matrix products, arithmetic and copies ran while one was open for 0% of the time, Pallas kernels for 0%

commit v1 on v0

v1 whole, which is shorter than its diff:
```python
import functools

import jax
import jax.numpy as jnp
from jax import lax
from jax.experimental import pallas as pl
from jax.experimental.pallas import tpu as pltpu
from jax.sharding import PartitionSpec as P

AW = 128
NO = 24
K = 800
KP = 896
ROWS = 36
OUT_ROWS = 18
PACK = 256
HALF = 128
MESH = pl.DeviceIdType.MESH
F32 = jnp.float32
BF16 = jnp.bfloat16


def remote(src, dst, send, recv, device):
    return pltpu.make_async_remote_copy(
        src_ref=src,
        dst_ref=dst,
        send_sem=send,
        recv_sem=recv,
        device_id=device,
        device_id_type=MESH,
    )


def kernel(
    t_hbm, v_hbm, occ, virt, virt_row, out,
    t_in, v_in, v_cat, t_all, l_f32, lhs, part, core_in, plus_in, minus_in, z_in, total, flip, turned, pieces, done,
    local_sem, z_send, z_recv, xr_send, xr_recv, xl_send, xl_recv, fr_send, fr_recv, fl_send, fl_recv,
    c_send, c_recv, p_send, p_recv, m_send, m_recv, h_send, h_recv, r_send, r_recv, a_send, a_recv,
):
    m, k = lax.axis_index("ab"), lax.axis_index("cd")
    x, z = m // 4, m % 4
    y, zh, c = k // 4, (k // 2) % 2, k % 2
    xl, xr = (x + 3) % 4, (x + 1) % 4
    xf = (x + 2) % 4
    zs = (z, z + 1 - 2 * (z % 2), (z + 2) % 4, 3 - z)
    left, right = (xl * 4 + z, k), (xr * 4 + z, k)
    along_z = [(x * 4 + zs[d], k) for d in range(4)]
    sibling = (m, k + 1 - 2 * c)
    up = (m, ((y + 1) % 8) * 4 + k % 4)
    down = (m, ((y + 7) % 8) * 4 + k % 4)
    across = (m, k + 2 - 4 * zh)

    v_copy = pltpu.make_async_copy(v_hbm, v_in, local_sem.at[0])
    t_copy = pltpu.make_async_copy(t_hbm, t_in, local_sem.at[1])
    t_copy.start()
    v_copy.start()
    barrier = pltpu.get_barrier_semaphore()
    peers = (left, right, *along_z[1:], sibling, up, down, across)
    for peer in peers:
        pl.semaphore_signal(barrier, inc=1, device_id=peer, device_id_type=MESH)

    t_copy.wait()
    for j in range(6):
        t_all[m, pl.ds(ROWS * j, ROWS), :] = t_in[:, 128 * j : 128 * j + 128]
    t_all[m, pl.ds(ROWS * 6, PACK - ROWS * 6), :] = jnp.zeros((PACK - ROWS * 6, 128), F32)
    t_all[m, pl.ds(ROWS * 6, ROWS), 0:32] = t_in[:, 768:800]
    pl.semaphore_wait(barrier, len(peers))

    pending = []

    def go(copy):
        copy.start()
        pending.append(copy)

    def send_x(d):
        block = t_all.at[x * 4 + zs[d]]
        go(remote(block, block, xr_send.at[d], xr_recv.at[d], right))
        go(remote(block, block, xl_send.at[d], xl_recv.at[d], left))

    send_x(0)
    for d in range(1, 4):
        go(remote(t_all.at[m], t_all.at[m], z_send.at[d], z_recv.at[d], along_z[d]))

    v_copy.wait()
    for part_no in range(3):
        v_cat[pl.ds(part_no * KP + K, KP - K), :] = jnp.zeros((KP - K, 1024), BF16)

    def split_v(i, carry):
        rows = pl.ds(pl.multiple_of(i * 80, 80), 80)
        value = v_in[rows, :]
        high = value.astype(BF16)
        low = (value - high.astype(F32)).astype(BF16)
        v_cat[pl.ds(pl.multiple_of(i * 80, 16), 80), :] = high
        v_cat[pl.ds(pl.multiple_of(KP + i * 80, 16), 80), :] = high
        v_cat[pl.ds(pl.multiple_of(2 * KP + i * 80, 16), 80), :] = low
        return carry

    lax.fori_loop(0, K // 80, split_v, 0)
    l_f32[...] = jnp.zeros_like(l_f32)

    def from_z(d):
        block = t_all.at[x * 4 + zs[d]]
        remote(block, block, z_send.at[d], z_recv.at[d], along_z[d]).wait_recv()
        send_x(d)

    def from_x(d):
        block = t_all.at[xl * 4 + zs[d]]
        remote(block, block, xr_send.at[d], xr_recv.at[d], right).wait_recv()
        piece = t_all.at[xl * 4 + zs[d], pl.ds(0, HALF)]
        go(remote(piece, piece, fr_send.at[d], fr_recv.at[d], right))
        block = t_all.at[xr * 4 + zs[d]]
        remote(block, block, xl_send.at[d], xl_recv.at[d], left).wait_recv()
        piece = t_all.at[xr * 4 + zs[d], pl.ds(HALF, HALF)]
        go(remote(piece, piece, fl_send.at[d], fl_recv.at[d], left))

    def group(g):
        for w in range(4):
            slot = g * 4 + w
            for j in range(7):
                l_f32[pl.ds(40 * w, ROWS), 128 * j : 128 * j + 128] = t_all[slot, pl.ds(ROWS * j, ROWS), :]
        value = l_f32[...]
        high = value.astype(BF16)
        lhs[:, 0:KP] = high
        lhs[:, KP : 2 * KP] = (value - high.astype(F32)).astype(BF16)
        lhs[:, 2 * KP : 3 * KP] = high
        for n in range(4):
            product = jnp.dot(lhs[...], v_cat[:, 256 * n : 256 * n + 256], preferred_element_type=F32)
            for w in range(4):
                for h in range(2):
                    part[g * 4 + w, :, 2 * n + h, :] = product[40 * w : 40 * w + ROWS, 128 * h : 128 * h + 128]
        for w in range(4):
            s = g * 4 + w
            go(
                remote(
                    part.at[s, pl.ds(OUT_ROWS * (1 - c), OUT_ROWS)], core_in.at[s],
                    c_send.at[s], c_recv.at[s], sibling,
                )
            )

    from_z(1)
    from_x(0)
    from_z(2)
    from_z(3)
    from_x(1)
    group(x)
    from_x(2)
    from_x(3)
    group(xl)
    group(xr)
    for d in range(4):
        piece = t_all.at[xf * 4 + zs[d], pl.ds(0, HALF)]
        remote(piece, piece, fr_send.at[d], fr_recv.at[d], right).wait_recv()
        piece = t_all.at[xf * 4 + zs[d], pl.ds(HALF, HALF)]
        remote(piece, piece, fl_send.at[d], fl_recv.at[d], left).wait_recv()
    group(xf)

    kind = (1 - zh, zh)

    def own(s):
        mine = pl.ds(OUT_ROWS * c, OUT_ROWS)
        remote(core_in.at[s], core_in.at[s], c_send.at[s], c_recv.at[s], sibling).wait_recv()
        part[s, mine] = part[s, mine] + core_in[s]

    for e in range(2):
        s = ((y + 4) % 8) * 2 + kind[e]
        own(s)
        go(remote(part.at[s, pl.ds(OUT_ROWS * c, 9)], plus_in.at[0, e, pl.ds(0, 9)], p_send.at[0, e], p_recv.at[0, e], up))
        go(remote(part.at[s, pl.ds(OUT_ROWS * c + 9, 9)], minus_in.at[0, e, pl.ds(9, 9)], m_send.at[0, e], m_recv.at[0, e], down))
    for step in range(1, 4):
        for e in range(2):
            for sign in (1, -1):
                into = plus_in if sign == 1 else minus_in
                send, recv, to = (p_send, p_recv, up) if sign == 1 else (m_send, m_recv, down)
                s = ((y + 8 + sign * (4 - step)) % 8) * 2 + kind[e]
                own(s)
                first, count = (0, OUT_ROWS) if step > 1 else (0, 9) if sign == 1 else (9, 9)
                arrived = into.at[step - 1, e, pl.ds(first, count)]
                remote(arrived, arrived, send.at[step - 1, e], recv.at[step - 1, e], to).wait_recv()
                mine = pl.ds(OUT_ROWS * c + first, count)
                part[s, mine] = part[s, mine] + into[step - 1, e, pl.ds(first, count)]
                go(remote(part.at[s, pl.ds(OUT_ROWS * c, OUT_ROWS)], into.at[step, e], send.at[step, e], recv.at[step, e], to))
    for e in range(2):
        s = y * 2 + kind[e]
        own(s)
        remote(plus_in.at[3, e], plus_in.at[3, e], p_send.at[3, e], p_recv.at[3, e], up).wait_recv()
        remote(minus_in.at[3, e], minus_in.at[3, e], m_send.at[3, e], m_recv.at[3, e], down).wait_recv()
        total[e] = part[s, pl.ds(OUT_ROWS * c, OUT_ROWS)] + (plus_in[3, e] + minus_in[3, e])
        if e == 0:
            go(remote(total.at[0], z_in, h_send.at[0], h_recv.at[0], across))
    remote(z_in, z_in, h_send.at[0], h_recv.at[0], across).wait_recv()
    total[1] = total[1] + z_in[...]

    flip[pl.ds(OUT_ROWS, 32 - OUT_ROWS)] = jnp.zeros((32 - OUT_ROWS, 8, 128), F32)

    def mirrored(r):
        row = k * OUT_ROWS + r
        other = (row % NO) * NO + row // NO
        return other // OUT_ROWS, other % OUT_ROWS

    def row_copy(r):
        owner, place = mirrored(r)
        return remote(total.at[1, r], flip.at[place], r_send.at[r], r_recv.at[place], (m, owner))

    def send_row(r, carry):
        owner, place = mirrored(r)

        @pl.when(owner != k)
        def _():
            row_copy(r).start()

        @pl.when(owner == k)
        def _():
            flip[place] = total[1, r]

        return carry

    lax.fori_loop(0, OUT_ROWS, send_row, 0)

    def wait_row(r, carry):
        owner, place = mirrored(r)

        @pl.when(owner != k)
        def _():
            remote(flip.at[r], flip.at[r], r_send.at[r], r_recv.at[r], (m, owner)).wait_recv()

        return carry

    lax.fori_loop(0, OUT_ROWS, wait_row, 0)

    turned[...] = flip[...].reshape(256, 128).T.reshape(16, 8, 256)
    pieces[m] = turned[m]

    def send_piece(d, carry):
        to = (m + d) % 16
        remote(turned.at[to], pieces.at[m], a_send.at[d], a_recv.at[d], (to, k)).start()
        return carry

    lax.fori_loop(1, 16, send_piece, 0)

    lane = lax.broadcasted_iota(jnp.int32, (8, 128), 1)
    sublane = lax.broadcasted_iota(jnp.int32, (8, 128), 0)
    energy = jnp.zeros((8, 128), F32)
    for q in range(8):
        energy = jnp.where(sublane == q, virt[m * 8 + q], energy)
    energy = energy + jnp.broadcast_to(virt_row[...], (8, 128))

    def wait_piece(d, carry):
        source = (m + 16 - d) % 16
        remote(pieces.at[source], pieces.at[source], a_send.at[d], a_recv.at[d], (source, k)).wait_recv()
        return carry

    lax.fori_loop(1, 16, wait_piece, 0)

    low = [pltpu.roll(pieces[q, :, 0:128], 8 * q, 1) if q else pieces[q, :, 0:128] for q in range(16)]
    top = [pltpu.roll(pieces[q, :, 128:256], 8 * q, 1) if q else pieces[q, :, 128:256] for q in range(16)]
    for r in range(OUT_ROWS):
        have = low if r < 16 else top
        shift = r % 16
        mixed = have[0]
        for q in range(1, 16):
            mixed = jnp.where(lane // 8 == (shift + q) % 16, have[q], mixed)
        mirror = pltpu.roll(mixed, 128 - 8 * shift, 1) if shift else mixed
        row = k * OUT_ROWS + r
        below = occ[row // NO] + occ[row % NO]
        done[r] = (total[1, r] + mirror) / (energy - below)
    for q in range(8):
        out[:, 128 * q : 128 * q + 128] = done[:, q, :]

    for copy in pending:
        copy.wait_send()

    def done_row(r, carry):
        owner, place = mirrored(r)

        @pl.when(owner != k)
        def _():
            row_copy(r).wait_send()

        return carry

    lax.fori_loop(0, OUT_ROWS, done_row, 0)

    def done_piece(d, carry):
        to = (m + d) % 16
        remote(turned.at[to], pieces.at[m], a_send.at[d], a_recv.at[d], (to, k)).wait_send()
        return carry

    lax.fori_loop(1, 16, done_piece, 0)


def body(amplitudes, integrals, occupied_energy, virtual_energy):
    dma = pltpu.SemaphoreType.DMA
    call = pl.pallas_call(
        kernel,
        out_shape=jax.ShapeDtypeStruct((OUT_ROWS, 1024), F32),
        in_specs=[
            pl.BlockSpec(memory_space=pltpu.HBM),
            pl.BlockSpec(memory_space=pltpu.HBM),
            pl.BlockSpec(memory_space=pltpu.SMEM),
            pl.BlockSpec(memory_space=pltpu.SMEM),
            pl.BlockSpec(memory_space=pltpu.VMEM),
        ],
        out_specs=pl.BlockSpec(memory_space=pltpu.VMEM),
        scratch_shapes=[
            pltpu.VMEM((ROWS, K), F32),
            pltpu.VMEM((K, 1024), F32),
            pltpu.VMEM((3 * KP, 1024), BF16),
            pltpu.VMEM((16, PACK, 128), F32),
            pltpu.VMEM((160, KP), F32),
            pltpu.VMEM((160, 3 * KP), BF16),
            pltpu.VMEM((16, ROWS, 8, 128), F32),
            pltpu.VMEM((16, OUT_ROWS, 8, 128), F32),
            pltpu.VMEM((4, 2, OUT_ROWS, 8, 128), F32),
            pltpu.VMEM((4, 2, OUT_ROWS, 8, 128), F32),
            pltpu.VMEM((OUT_ROWS, 8, 128), F32),
            pltpu.VMEM((2, OUT_ROWS, 8, 128), F32),
            pltpu.VMEM((32, 8, 128), F32),
            pltpu.VMEM((16, 8, 256), F32),
            pltpu.VMEM((16, 8, 256), F32),
            pltpu.VMEM((OUT_ROWS, 8, 128), F32),
            dma((2,)),
            dma((4,)), dma((4,)),
            dma((4,)), dma((4,)), dma((4,)), dma((4,)),
            dma((4,)), dma((4,)), dma((4,)), dma((4,)),
            dma((16,)), dma((16,)),
            dma((4, 2)), dma((4, 2)), dma((4, 2)), dma((4, 2)),
            dma((1,)), dma((1,)),
            dma((OUT_ROWS,)), dma((OUT_ROWS,)),
            dma((16,)), dma((16,)),
        ],
        compiler_params=pltpu.CompilerParams(
            collective_id=0, has_side_effects=True, vmem_limit_bytes=48 * 1024 * 1024
        ),
    )
    return call(
        amplitudes,
        integrals.T,
        occupied_energy,
        virtual_energy,
        virtual_energy.reshape(1, AW),
    )


def solution(mesh):
    return jax.shard_map(
        body,
        mesh=mesh,
        in_specs=(P("ab", "cd"), P("ab", "cd"), P(), P()),
        out_specs=P("cd", "ab"),
        check_vma=False,
    )
```

time: 383 us -> 81.6 us (0.21)
  the two profiles are of different devices: /device:TPU:19 before, /device:TPU:1 now
where the time goes in v1:
time: 81.6 us; the launch traced here: 81.5 us
  Pallas kernels  76.7 us (94%)
  local copies, waits for them, and re-layouts  4.79 us (6%)
    pallas_call x1, Pallas kernels, body(): call(amplitudes, integrals.T, occupied_energy, virtual_energy, virtual_en...  76.7 us
    unnamed x9, local copies, waits for them, and re-layouts  4.79 us

profile of v1, /device:TPU:1, one launch (start us, length us, event | category | flops | bytes accessed | tf_op | source)
XLA Modules:
  0.0 81.5 jit_solution(2367966952681375614)
XLA Ops:
  0.0 0.0 copy-start
  0.0 1.9 %copy-done = f32[1024,800]{0,1:T(8,128)S(1)} copy-done((f32[1024,800]{0,1:T(8,128)S(1)}, f32[1024,800]{0,1:T(8,128)}, u32[]{:S(2)}) %copy-start) | copy-done | bytes 3276824
  1.9 0.0 copy-start.1
  1.9 0.9 %copy-done.1 = f32[36,800]{1,0:T(8,128)S(1)} copy-done((f32[36,800]{1,0:T(8,128)S(1)}, f32[36,800]{1,0:T(8,128)}, u32[]{:S(2)}) %copy-start.1) | copy-done | bytes 115224
  2.8 0.0 copy-start.2
  2.8 0.7 copy-done.2
  3.5 0.0 copy-start.3
  3.5 0.7 copy-done.3
  4.1 76.7 %shard_map.46 = f32[18,1024]{1,0:T(8,128)S(1)} custom-call(f32[36,800]{1,0:T(8,128)S(1)} %copy-done.1, f32[800,1024]{1,0:T(8,128)S(1)} %bitcast.2, f32[24]{0:T(128)S(1)} %copy-done.3, f32[128]{0:T(128)S(1)} %copy-done.2, f32[1,128]{1,0:T(1,128)S(1)} %bitcast.3), custom_call_target="tpu_custom_call" | custom-call | tf_op jit(solution)/shard_map/pallas_call | solution.py:335
  80.8 0.6 copy.6
Async XLA Ops:
  0.0 1.9 %copy-start = (f32[1024,800]{0,1:T(8,128)S(1)}, f32[1024,800]{0,1:T(8,128)}, u32[]{:S(2)}) copy-start(f32[1024,800]{0,1:T(8,128)} %param.5) | copy-start | bytes 9830404
  1.9 0.9 %copy-start.1 = (f32[36,800]{1,0:T(8,128)S(1)}, f32[36,800]{1,0:T(8,128)}, u32[]{:S(2)}) copy-start(f32[36,800]{1,0:T(8,128)} %t_hbm.1) | copy-start | bytes 345604
  2.8 0.7 copy-start.2
  3.5 0.7 copy-start.3

commit v2 on v0

v2 whole, which is shorter than its diff:
```python
import functools

import jax
import jax.numpy as jnp
from jax import lax
from jax.experimental import pallas as pl
from jax.experimental.pallas import tpu as pltpu
from jax.sharding import PartitionSpec as P

AW = 128
NO = 24
K = 800
KP = 896
ROWS = 36
OUT_ROWS = 18
PACK = 232
TAIL = 9
CUTS = ((0, 56), (56, 64), (120, 56), (176, 56))
MESH = pl.DeviceIdType.MESH
F32 = jnp.float32
BF16 = jnp.bfloat16


def remote(src, dst, send, recv, device):
    return pltpu.make_async_remote_copy(
        src_ref=src,
        dst_ref=dst,
        send_sem=send,
        recv_sem=recv,
        device_id=device,
        device_id_type=MESH,
    )


def kernel(
    t_hbm, v_hbm, occ_hbm, virt_hbm, row_hbm, out,
    t_in, v_in, occ, virt, virt_row, v_cat, t_all, l_f32, lhs, part, core_in, plus_in, minus_in, z_in, total, flip,
    turned, pieces, done,
    local_sem, g_send, g_recv,
    c_send, c_recv, p_send, p_recv, m_send, m_recv, h_send, h_recv, r_send, r_recv, a_send, a_recv,
):
    m, k = lax.axis_index("ab"), lax.axis_index("cd")
    x, z = lax.div(m, 4), lax.rem(m, 4)
    y, zh, c = lax.div(k, 4), lax.rem(lax.div(k, 2), 2), lax.rem(k, 2)
    xl, xr, xf = lax.rem(x + 3, 4), lax.rem(x + 1, 4), lax.rem(x + 2, 4)
    zs = (z, z + 1 - 2 * lax.rem(z, 2), lax.rem(z + 2, 4), 3 - z)
    near = lax.div(z, 2)
    left, right = (xl * 4 + z, k), (xr * 4 + z, k)
    along_z = [(x * 4 + zs[d], k) for d in range(4)]
    sibling = (m, k + 1 - 2 * c)
    up = (m, lax.rem(y + 1, 8) * 4 + lax.rem(k, 4))
    down = (m, lax.rem(y + 7, 8) * 4 + lax.rem(k, 4))
    across = (m, k + 2 - 4 * zh)

    t_copy = pltpu.make_async_copy(t_hbm, t_in, local_sem.at[0])
    t_copy.start()
    v_copy = pltpu.make_async_copy(v_hbm, v_in, local_sem.at[1])
    v_copy.start()
    small = [
        pltpu.make_async_copy(occ_hbm, occ, local_sem.at[2]),
        pltpu.make_async_copy(virt_hbm, virt, local_sem.at[3]),
        pltpu.make_async_copy(row_hbm, virt_row, local_sem.at[4]),
    ]
    for copy in small:
        copy.start()
    barrier = pltpu.get_barrier_semaphore()
    peers = (left, right, *along_z[1:], sibling, up, down, across)
    for peer in peers:
        pl.semaphore_signal(barrier, inc=1, device_id=peer, device_id_type=MESH)

    t_copy.wait()
    for j in range(6):
        t_all[m, pl.ds(ROWS * j, ROWS), :] = t_in[:, 128 * j : 128 * j + 128]
    t_all[m, pl.ds(ROWS * 6, TAIL), :] = jnp.concatenate(
        [t_in[TAIL * q : TAIL * q + TAIL, 768:800] for q in range(4)], axis=1
    )
    t_all[m, pl.ds(ROWS * 6 + TAIL, PACK - ROWS * 6 - TAIL), :] = jnp.zeros((PACK - ROWS * 6 - TAIL, 128), F32)
    pl.semaphore_wait(barrier, len(peers))

    pending = []

    def go(copy):
        copy.start()
        pending.append(copy)

    def await_into(ref, send, recv, device):
        remote(ref, ref, send, recv, device).wait_recv()

    xs = (x, xl, xr, xf)
    links = {"right": right, "left": left, "z1": along_z[1], "z2": along_z[2], "z3": along_z[3]}
    sent = {}

    def place_at(way, g, d):
        if way == "right":
            return (1 if g == 0 else 3), d
        if way == "left":
            return (2 if g == 0 else 3), d
        return g, d ^ int(way[1])

    def give(way, g, d, q):
        there, depth = place_at(way, g, d)
        number = sent.setdefault((way, g, d), [len(sent), []])
        number[1].append(q)
        piece = t_all.at[xs[g] * 4 + zs[d], pl.ds(*CUTS[q])]
        remote(piece, piece, g_send.at[number[0]], g_recv.at[there * 4 + depth, q], links[way]).start()

    def take(g, d, q):
        await_into(t_all.at[xs[g] * 4 + zs[d], pl.ds(*CUTS[q])], g_send.at[0], g_recv.at[g * 4 + d, q], right)

    def give_x(d, q):
        give("right", 0, d, q)
        give("left", 0, d, q)

    def from_sides(d, q):
        take(1, d, q)
        if q < 2:
            give("right", 1, d, q)
        take(2, d, q)
        if q >= 2:
            give("left", 2, d, q)

    every = range(4)
    for way in ("right", "left", "z1", "z2", "z3"):
        for q in every:
            give(way, 0, 0, q)

    l_f32[...] = jnp.zeros_like(l_f32)
    for part_no in range(2):
        v_cat[pl.ds(part_no * KP + K, KP - K), :] = jnp.zeros((KP - K, 1024), BF16)
    v_copy.wait()

    def split_v(i, carry):
        value = v_in[pl.ds(pl.multiple_of(i * 80, 80), 80), :]
        high = value.astype(BF16)
        low = (value - high.astype(F32)).astype(BF16)
        v_cat[pl.ds(pl.multiple_of(i * 80, 16), 80), :] = high
        v_cat[pl.ds(pl.multiple_of(KP + i * 80, 16), 80), :] = low
        return carry

    lax.fori_loop(0, K // 80, split_v, 0)
    def multiply(slots):
        many = len(slots)
        for w, slot in enumerate(slots):
            for j in range(6):
                l_f32[pl.ds(40 * w, ROWS), 128 * j : 128 * j + 128] = t_all[slot, pl.ds(ROWS * j, ROWS), :]
            for q in range(4):
                l_f32[pl.ds(40 * w + TAIL * q, TAIL), 768:800] = t_all[slot, pl.ds(ROWS * 6, TAIL), 32 * q : 32 * q + 32]
        size = 40 * many
        value = l_f32[0:size, :]
        high = value.astype(BF16)
        lhs[0:size, :] = high
        lhs[size : 2 * size, :] = (value - high.astype(F32)).astype(BF16)
        for n in range(4):
            both = jnp.dot(lhs[0 : 2 * size, :], v_cat[0:KP, 256 * n : 256 * n + 256], preferred_element_type=F32)
            rest = jnp.dot(lhs[0:size, :], v_cat[KP : 2 * KP, 256 * n : 256 * n + 256], preferred_element_type=F32)
            product = both[0:size] + (both[size : 2 * size] + rest)
            for w, slot in enumerate(slots):
                for h in range(2):
                    part[slot, :, 2 * n + h, :] = product[40 * w : 40 * w + ROWS, 128 * h : 128 * h + 128]
        for slot in slots:
            share = part.at[slot, pl.ds(OUT_ROWS * (1 - c), OUT_ROWS)]
            go(remote(share, core_in.at[slot], c_send.at[slot], c_recv.at[slot], sibling))

    for q in every:
        from_sides(0, q)
        if q >= 2:
            give("z1", 1, 0, q)
            give("z1", 2, 0, q)
    for q in (0, 1):
        take(0, 1, q)
        give_x(1, q)
    for q in every:
        take(0, 2, q)
        give_x(2, q)
    for q in every:
        from_sides(1, q)
    for q in every:
        take(0, 3, q)
        give_x(3, q)
    for q in every:
        from_sides(2, q)
    for q in (2, 3):
        take(0, 1, q)
    multiply([x * 4 + w for w in range(4)])
    for q in every:
        from_sides(3, q)
    multiply([xl * 4 + w for w in range(4)])
    multiply([xr * 4 + w for w in range(4)])
    for d in (0, 1):
        for q in every:
            take(3, d, q)
    multiply([xf * 4 + 2 * near, xf * 4 + 2 * near + 1])
    for d in (2, 3):
        for q in every:
            take(3, d, q)
    multiply([xf * 4 + 2 - 2 * near, xf * 4 + 3 - 2 * near])

    kind = (1 - zh, zh)

    def own(s):
        await_into(core_in.at[s], c_send.at[s], c_recv.at[s], sibling)
        mine = pl.ds(OUT_ROWS * c, OUT_ROWS)
        part[s, mine] = part[s, mine] + core_in[s]

    ways = ((1, plus_in, p_send, p_recv, up), (-1, minus_in, m_send, m_recv, down))
    nine = (pl.ds(0, 9), pl.ds(9, 9))

    def share_of(s, h):
        return part.at[s, pl.ds(OUT_ROWS * c + 9 * h, 9)]

    for e in range(2):
        s = lax.rem(y + 4, 8) * 2 + kind[e]
        own(s)
        for h, (_, into, send, recv, to) in enumerate(ways):
            go(remote(share_of(s, h), into.at[0, e, nine[h]], send.at[0, e, h], recv.at[0, e, h], to))
    for step in range(1, 4):
        for e in range(2):
            owners = [lax.rem(y + 8 + sign * (4 - step), 8) * 2 + kind[e] for sign in (1, -1)]
            for s in owners:
                own(s)
            for h in range(2):
                for turn, (s, (_, into, send, recv, to)) in enumerate(zip(owners, ways)):
                    if step > 1 or h == turn:
                        await_into(into.at[step - 1, e, nine[h]], send.at[step - 1, e, h], recv.at[step - 1, e, h], to)
                        mine = pl.ds(OUT_ROWS * c + 9 * h, 9)
                        part[s, mine] = part[s, mine] + into[step - 1, e, nine[h]]
                    go(remote(share_of(s, h), into.at[step, e, nine[h]], send.at[step, e, h], recv.at[step, e, h], to))
    for e in range(2):
        s = y * 2 + kind[e]
        own(s)
        for h in range(2):
            for _, into, send, recv, to in ways:
                await_into(into.at[3, e, nine[h]], send.at[3, e, h], recv.at[3, e, h], to)
            total[e, nine[h]] = part[s, pl.ds(OUT_ROWS * c + 9 * h, 9)] + (plus_in[3, e, nine[h]] + minus_in[3, e, nine[h]])
            if e == 0:
                go(remote(total.at[0, nine[h]], z_in.at[nine[h]], h_send.at[h], h_recv.at[h], across))

    i0 = lax.div(k * OUT_ROWS, NO)
    j0 = k * OUT_ROWS - i0 * NO

    def indices(r):
        wrap = jnp.where(j0 + r >= NO, 1, 0)
        return i0 + wrap, j0 + r - NO * wrap

    def mirrored(r):
        i, j = indices(r)
        other = j * NO + i
        owner = lax.div(other * 3641, 65536)
        return owner, other - owner * OUT_ROWS

    def row_copy(r, owner, place):
        return remote(total.at[1, r], flip.at[place], r_send.at[r], r_recv.at[place], (m, owner))

    def send_row(r, carry):
        owner, place = mirrored(r)

        @pl.when(owner != k)
        def _():
            row_copy(r, owner, place).start()

        @pl.when(owner == k)
        def _():
            flip[place] = total[1, r]

        return carry

    for h in range(2):
        await_into(z_in.at[nine[h]], h_send.at[h], h_recv.at[h], across)
        total[1, nine[h]] = total[1, nine[h]] + z_in[nine[h]]
        lax.fori_loop(9 * h, 9 * h + 9, send_row, 0)

    flip[pl.ds(OUT_ROWS, 32 - OUT_ROWS)] = jnp.zeros((32 - OUT_ROWS, 8, 128), F32)
    for copy in small:
        copy.wait()
    lane = lax.broadcasted_iota(jnp.int32, (8, 128), 1)
    sublane = lax.broadcasted_iota(jnp.int32, (8, 128), 0)
    energy = jnp.zeros((8, 128), F32)
    for q in range(8):
        energy = jnp.where(sublane == q, virt[m * 8 + q], energy)
    energy = energy + jnp.broadcast_to(virt_row[...], (8, 128))
    for copy in pending:
        copy.wait_send()

    for (way, g, d), (number, pieces_sent) in sent.items():
        first, last = min(pieces_sent), max(pieces_sent)
        start = CUTS[first][0]
        span = t_all.at[xs[g] * 4 + zs[d], pl.ds(start, sum(CUTS[last]) - start)]
        remote(span, span, g_send.at[number], g_recv.at[0, 0], links[way]).wait_send()

    def wait_row(r, carry):
        owner, place = mirrored(r)

        @pl.when(owner != k)
        def _():
            await_into(flip.at[r], r_send.at[r], r_recv.at[r], (m, owner))
            row_copy(r, owner, place).wait_send()

        return carry

    lax.fori_loop(0, OUT_ROWS, wait_row, 0)

    turned[...] = flip[...].reshape(256, 128).T.reshape(16, 8, 256)

    def piece_copy(d):
        to = lax.rem(m + d, 16)
        return remote(turned.at[to], pieces.at[m], a_send.at[d], a_recv.at[d], (to, k))

    def send_piece(d, carry):
        piece_copy(d).start()
        return carry

    lax.fori_loop(1, 16, send_piece, 0)
    pieces[m] = turned[m]

    def wait_piece(d, carry):
        source = lax.rem(m + 16 - d, 16)
        await_into(pieces.at[source], a_send.at[d], a_recv.at[d], (source, k))
        piece_copy(d).wait_send()
        return carry

    lax.fori_loop(1, 16, wait_piece, 0)

    low = [pltpu.roll(pieces[q, :, 0:128], 8 * q, 1) if q else pieces[q, :, 0:128] for q in range(16)]
    top = [pltpu.roll(pieces[q, :, 128:256], 8 * q, 1) if q else pieces[q, :, 128:256] for q in range(16)]
    for r in range(OUT_ROWS):
        have = low if r < 16 else top
        shift = r % 16
        mixed = have[0]
        for q in range(1, 16):
            mixed = jnp.where(lane // 8 == (shift + q) % 16, have[q], mixed)
        mirror = pltpu.roll(mixed, 128 - 8 * shift, 1) if shift else mixed
        i, j = indices(r)
        done[r] = (total[1, r] + mirror) / (energy - (occ[i] + occ[j]))
    for q in range(8):
        out[:, 128 * q : 128 * q + 128] = done[:, q, :]


def body(amplitudes, integrals, occupied_energy, virtual_energy):
    dma = pltpu.SemaphoreType.DMA
    call = pl.pallas_call(
        kernel,
        out_shape=jax.ShapeDtypeStruct((OUT_ROWS, 1024), F32),
        in_specs=[pl.BlockSpec(memory_space=pltpu.HBM)] * 5,
        out_specs=pl.BlockSpec(memory_space=pltpu.VMEM),
        scratch_shapes=[
            pltpu.VMEM((ROWS, K), F32),
            pltpu.VMEM((K, 1024), F32),
            pltpu.SMEM((NO,), F32),
            pltpu.SMEM((AW,), F32),
            pltpu.VMEM((1, AW), F32),
            pltpu.VMEM((2 * KP, 1024), BF16),
            pltpu.VMEM((16, PACK, 128), F32),
            pltpu.VMEM((160, KP), F32),
            pltpu.VMEM((320, KP), BF16),
            pltpu.VMEM((16, ROWS, 8, 128), F32),
            pltpu.VMEM((16, OUT_ROWS, 8, 128), F32),
            pltpu.VMEM((4, 2, OUT_ROWS, 8, 128), F32),
            pltpu.VMEM((4, 2, OUT_ROWS, 8, 128), F32),
            pltpu.VMEM((OUT_ROWS, 8, 128), F32),
            pltpu.VMEM((2, OUT_ROWS, 8, 128), F32),
            pltpu.VMEM((32, 8, 128), F32),
            pltpu.VMEM((16, 8, 256), F32),
            pltpu.VMEM((16, 8, 256), F32),
            pltpu.VMEM((OUT_ROWS, 8, 128), F32),
            dma((5,)),
            dma((21,)), dma((16, 4)),
            dma((16,)), dma((16,)),
            dma((4, 2, 2)), dma((4, 2, 2)), dma((4, 2, 2)), dma((4, 2, 2)),
            dma((2,)), dma((2,)),
            dma((OUT_ROWS,)), dma((OUT_ROWS,)),
            dma((16,)), dma((16,)),
        ],
        compiler_params=pltpu.CompilerParams(
            collective_id=0, has_side_effects=True, vmem_limit_bytes=48 * 1024 * 1024
        ),
    )
    return call(
        *(
            pltpu.with_memory_space_constraint(value, pltpu.HBM)
            for value in (
                amplitudes,
                integrals.T,
                occupied_energy,
                virtual_energy,
                virtual_energy.reshape(1, AW),
            )
        )
    )


def solution(mesh):
    return jax.shard_map(
        body,
        mesh=mesh,
        in_specs=(P("ab", "cd"), P("ab", "cd"), P(), P()),
        out_specs=P("cd", "ab"),
        check_vma=False,
    )
```

time: 383 us -> 72.2 us (0.19)
  the two profiles are of different devices: /device:TPU:19 before, /device:TPU:1 now
where the time goes in v2:
time: 72.2 us; the launch traced here: 71.9 us
  Pallas kernels  71.3 us (99%)
    pallas_call x1, Pallas kernels, body(): call(*(pltpu.with_memory_space_constraint(value, pltpu.HBM) for value in...  71.3 us

profile of v2, /device:TPU:1, one launch (start us, length us, event | category | flops | bytes accessed | tf_op | source)
XLA Modules:
  0.0 71.9 jit_solution(11010931296621443200)
XLA Ops:
  0.0 71.3 %shard_map.46 = f32[18,1024]{1,0:T(8,128)S(1)} custom-call(f32[36,800]{1,0:T(8,128)} %t_hbm.1, f32[800,1024]{1,0:T(8,128)} %bitcast.2, f32[24]{0:T(128)} %occ_hbm.1, f32[128]{0:T(128)} %virt_hbm.1, f32[1,128]{1,0:T(1,128)} %bitcast.3), custom_call_target="tpu_custom_call" | custom-call | tf_op jit(solution)/shard_map/pallas_call | solution.py:377
  71.3 0.6 copy.6

commit v3 on v2

--- a/solution.py
+++ b/solution.py
@@ -208,23 +208,56 @@
     def share_of(s, h):
         return part.at[s, pl.ds(OUT_ROWS * c + 9 * h, 9)]
 
-    for e in range(2):
-        s = lax.rem(y + 4, 8) * 2 + kind[e]
-        own(s)
-        for h, (_, into, send, recv, to) in enumerate(ways):
-            go(remote(share_of(s, h), into.at[0, e, nine[h]], send.at[0, e, h], recv.at[0, e, h], to))
-    for step in range(1, 4):
+    def owner(way, step, e):
+        return lax.rem(y + 8 + (4 - step) * ways[way][0], 8) * 2 + kind[e]
+
+    def hop(way, step, e, h):
+        _, into, send, recv, to = ways[way]
+        s = owner(way, step, e)
+        if step > (0 if h == way else 1):
+            await_into(into.at[step - 1, e, nine[h]], send.at[step - 1, e, h], recv.at[step - 1, e, h], to)
+            mine = pl.ds(OUT_ROWS * c + 9 * h, 9)
+            part[s, mine] = part[s, mine] + into[step - 1, e, nine[h]]
+        go(remote(share_of(s, h), into.at[step, e, nine[h]], send.at[step, e, h], recv.at[step, e, h], to))
+
+    for step in range(4):
         for e in range(2):
-            owners = [lax.rem(y + 8 + sign * (4 - step), 8) * 2 + kind[e] for sign in (1, -1)]
-            for s in owners:
-                own(s)
-            for h in range(2):
-                for turn, (s, (_, into, send, recv, to)) in enumerate(zip(owners, ways)):
-                    if step > 1 or h == turn:
-                        await_into(into.at[step - 1, e, nine[h]], send.at[step - 1, e, h], recv.at[step - 1, e, h], to)
-                        mine = pl.ds(OUT_ROWS * c + 9 * h, 9)
-                        part[s, mine] = part[s, mine] + into[step - 1, e, nine[h]]
-                    go(remote(share_of(s, h), into.at[step, e, nine[h]], send.at[step, e, h], recv.at[step, e, h], to))
+            if step == 0:
+                own(owner(0, 0, e))
+            for way in range(2):
+                hop(way, step, e, way)
+            if step < 3:
+                for way in range(2):
+                    own(owner(way, step + 1, e))
+                    hop(way, step + 1, e, 1 - way)
+    holders = (k + 2 - 4 * zh, k)
+    starts = [lax.div(kk * OUT_ROWS, NO) for kk in holders]
+
+    def indices(e, r):
+        j = holders[e] * OUT_ROWS - starts[e] * NO + r
+        wrap = jnp.where(j >= NO, 1, 0)
+        return starts[e] + wrap, j - NO * wrap
+
+    def mirrored(e, r):
+        i, j = indices(e, r)
+        other = j * NO + i
+        holder = lax.div(other * 3641, 65536)
+        return holder, other - holder * OUT_ROWS
+
+    def row_copy(e, r, holder, place):
+        return remote(total.at[e, r], flip.at[zh, place], r_send.at[e, r], r_recv.at[zh, place], (m, holder))
+
+    def send_row(e, r):
+        holder, place = mirrored(e, r)
+
+        @pl.when(holder != k)
+        def _():
+            row_copy(e, r, holder, place).start()
+
+        @pl.when(holder == k)
+        def _():
+            flip[zh, place] = total[e, r]
+
     for e in range(2):
         s = y * 2 + kind[e]
         own(s)
@@ -235,41 +268,12 @@
             if e == 0:
                 go(remote(total.at[0, nine[h]], z_in.at[nine[h]], h_send.at[h], h_recv.at[h], across))
 
-    i0 = lax.div(k * OUT_ROWS, NO)
-    j0 = k * OUT_ROWS - i0 * NO
-
-    def indices(r):
-        wrap = jnp.where(j0 + r >= NO, 1, 0)
-        return i0 + wrap, j0 + r - NO * wrap
-
-    def mirrored(r):
-        i, j = indices(r)
-        other = j * NO + i
-        owner = lax.div(other * 3641, 65536)
-        return owner, other - owner * OUT_ROWS
-
-    def row_copy(r, owner, place):
-        return remote(total.at[1, r], flip.at[place], r_send.at[r], r_recv.at[place], (m, owner))
-
-    def send_row(r, carry):
-        owner, place = mirrored(r)
-
-        @pl.when(owner != k)
-        def _():
-            row_copy(r, owner, place).start()
-
-        @pl.when(owner == k)
-        def _():
-            flip[place] = total[1, r]
-
-        return carry
-
-    for h in range(2):
-        await_into(z_in.at[nine[h]], h_send.at[h], h_recv.at[h], across)
-        total[1, nine[h]] = total[1, nine[h]] + z_in[nine[h]]
-        lax.fori_loop(9 * h, 9 * h + 9, send_row, 0)
-
-    flip[pl.ds(OUT_ROWS, 32 - OUT_ROWS)] = jnp.zeros((32 - OUT_ROWS, 8, 128), F32)
+            def send_rows(r, carry, e=e):
+                send_row(e, r)
+                return carry
+
+            lax.fori_loop(9 * h, 9 * h + 9, send_rows, 0)
+
     for copy in small:
         copy.wait()
     lane = lax.broadcasted_iota(jnp.int32, (8, 128), 1)
@@ -288,18 +292,21 @@
         remote(span, span, g_send.at[number], g_recv.at[0, 0], links[way]).wait_send()
 
     def wait_row(r, carry):
-        owner, place = mirrored(r)
-
-        @pl.when(owner != k)
-        def _():
-            await_into(flip.at[r], r_send.at[r], r_recv.at[r], (m, owner))
-            row_copy(r, owner, place).wait_send()
+        natural, _ = mirrored(1, r)
+        for side in range(2):
+            source = natural + 2 * (side - lax.rem(lax.div(natural, 2), 2))
+
+            @pl.when(source != k)
+            def _():
+                await_into(flip.at[side, r], r_send.at[0, 0], r_recv.at[side, r], (m, source))
 
         return carry
 
     lax.fori_loop(0, OUT_ROWS, wait_row, 0)
 
-    turned[...] = flip[...].reshape(256, 128).T.reshape(16, 8, 256)
+    rows = flip[0] + flip[1]
+    filled = jnp.concatenate([rows, jnp.zeros((32 - OUT_ROWS, 8, 128), F32)], axis=0)
+    turned[...] = filled.reshape(256, 128).T.reshape(16, 8, 256)
 
     def piece_copy(d):
         to = lax.rem(m + d, 16)
@@ -311,6 +318,20 @@
 
     lax.fori_loop(1, 16, send_piece, 0)
     pieces[m] = turned[m]
+
+    def left_row(r, carry):
+        for e in range(2):
+            holder, place = mirrored(e, r)
+
+            @pl.when(holder != k)
+            def _():
+                row_copy(e, r, holder, place).wait_send()
+
+        return carry
+
+    lax.fori_loop(0, OUT_ROWS, left_row, 0)
+    for h in range(2):
+        await_into(z_in.at[nine[h]], h_send.at[h], h_recv.at[h], across)
 
     def wait_piece(d, carry):
         source = lax.rem(m + 16 - d, 16)
@@ -329,8 +350,8 @@
         for q in range(1, 16):
             mixed = jnp.where(lane // 8 == (shift + q) % 16, have[q], mixed)
         mirror = pltpu.roll(mixed, 128 - 8 * shift, 1) if shift else mixed
-        i, j = indices(r)
-        done[r] = (total[1, r] + mirror) / (energy - (occ[i] + occ[j]))
+        i, j = indices(1, r)
+        done[r] = (total[1, r] + z_in[r] + mirror) / (energy - (occ[i] + occ[j]))
     for q in range(8):
         out[:, 128 * q : 128 * q + 128] = done[:, q, :]
 
@@ -358,7 +379,7 @@
             pltpu.VMEM((4, 2, OUT_ROWS, 8, 128), F32),
             pltpu.VMEM((OUT_ROWS, 8, 128), F32),
             pltpu.VMEM((2, OUT_ROWS, 8, 128), F32),
-            pltpu.VMEM((32, 8, 128), F32),
+            pltpu.VMEM((2, OUT_ROWS, 8, 128), F32),
             pltpu.VMEM((16, 8, 256), F32),
             pltpu.VMEM((16, 8, 256), F32),
             pltpu.VMEM((OUT_ROWS, 8, 128), F32),
@@ -367,7 +388,7 @@
             dma((16,)), dma((16,)),
             dma((4, 2, 2)), dma((4, 2, 2)), dma((4, 2, 2)), dma((4, 2, 2)),
             dma((2,)), dma((2,)),
-            dma((OUT_ROWS,)), dma((OUT_ROWS,)),
+            dma((2, OUT_ROWS)), dma((2, OUT_ROWS)),
             dma((16,)), dma((16,)),
         ],
         compiler_params=pltpu.CompilerParams(

time: 72.2 us -> 67.4 us (0.934)
  Pallas kernels: 71.3 us -> 66.3 us
    pallas_call x1, Pallas kernels: 71.3 us -> 66.3 us  [body(): call(*(pltpu.with_memory_space_constraint(value, pltpu.HBM) for value in...]
where the time goes in v3:
time: 67.4 us; the launch traced here: 67 us
  Pallas kernels  66.3 us (98%)
    pallas_call x1, Pallas kernels, body(): call(*(pltpu.with_memory_space_constraint(value, pltpu.HBM) for value in...  66.3 us

profile of v3, /device:TPU:1, one launch (start us, length us, event | category | flops | bytes accessed | tf_op | source)
XLA Modules:
  0.0 67.0 jit_solution(2077006234005705131)
XLA Ops:
  0.0 66.3 %shard_map.46 = f32[18,1024]{1,0:T(8,128)S(1)} custom-call(f32[36,800]{1,0:T(8,128)} %t_hbm.1, f32[800,1024]{1,0:T(8,128)} %bitcast.2, f32[24]{0:T(128)} %occ_hbm.1, f32[128]{0:T(128)} %virt_hbm.1, f32[1,128]{1,0:T(1,128)} %bitcast.3), custom_call_target="tpu_custom_call" | custom-call | tf_op jit(solution)/shard_map/pallas_call | solution.py:398
  66.3 0.6 copy.6

commit v4 on v3

--- a/solution.py
+++ b/solution.py
@@ -161,6 +161,10 @@
             share = part.at[slot, pl.ds(OUT_ROWS * (1 - c), OUT_ROWS)]
             go(remote(share, core_in.at[slot], c_send.at[slot], c_recv.at[slot], sibling))
 
+    def pair(g, d):
+        first = xs[g] * 4 + 2 * (near if d == 0 else 1 - near)
+        multiply([first, first + 1])
+
     for q in every:
         from_sides(0, q)
         if q >= 2:
@@ -172,6 +176,9 @@
     for q in every:
         take(0, 2, q)
         give_x(2, q)
+    for q in (2, 3):
+        take(0, 1, q)
+    pair(0, 0)
     for q in every:
         from_sides(1, q)
     for q in every:
@@ -179,21 +186,23 @@
         give_x(3, q)
     for q in every:
         from_sides(2, q)
-    for q in (2, 3):
-        take(0, 1, q)
-    multiply([x * 4 + w for w in range(4)])
+    pair(0, 1)
+    pair(1, 0)
+    pair(2, 0)
     for q in every:
         from_sides(3, q)
-    multiply([xl * 4 + w for w in range(4)])
-    multiply([xr * 4 + w for w in range(4)])
-    for d in (0, 1):
-        for q in every:
-            take(3, d, q)
-    multiply([xf * 4 + 2 * near, xf * 4 + 2 * near + 1])
-    for d in (2, 3):
-        for q in every:
-            take(3, d, q)
-    multiply([xf * 4 + 2 - 2 * near, xf * 4 + 3 - 2 * near])
+    pair(1, 1)
+    pair(2, 1)
+    for q in every:
+        take(3, 0, q)
+    for q in every:
+        take(3, 1, q)
+    pair(3, 0)
+    for q in every:
+        take(3, 2, q)
+    for q in every:
+        take(3, 3, q)
+    pair(3, 1)
 
     kind = (1 - zh, zh)
 

time: 67.4 us -> 66.8 us (level)
  no operation moved by 1% of the time
where the time goes in v4:
time: 66.8 us; the launch traced here: 66.7 us
  Pallas kernels  66.1 us (99%)
    pallas_call x1, Pallas kernels, body(): call(*(pltpu.with_memory_space_constraint(value, pltpu.HBM) for value in...  66.1 us

profile of v4, /device:TPU:1, one launch (start us, length us, event | category | flops | bytes accessed | tf_op | source)
XLA Modules:
  0.0 66.7 jit_solution(6491865534616767698)
XLA Ops:
  0.0 66.1 %shard_map.46 = f32[18,1024]{1,0:T(8,128)S(1)} custom-call(f32[36,800]{1,0:T(8,128)} %t_hbm.1, f32[800,1024]{1,0:T(8,128)} %bitcast.2, f32[24]{0:T(128)} %occ_hbm.1, f32[128]{0:T(128)} %virt_hbm.1, f32[1,128]{1,0:T(1,128)} %bitcast.3), custom_call_target="tpu_custom_call" | custom-call | tf_op jit(solution)/shard_map/pallas_call | solution.py:407
  66.1 0.6 copy.6
